TPU v7x, 32 devices: a whole 2x2x4 slice. The times are simulated.
32 devices in a mesh: grp: 4 (over z), shard: 8 (over y, x, core).
Axes of the slice: x: 2, y: 2, z: 4, core: 2. Of those that a mesh axis runs over, the one named last changes fastest.
Arguments:
- owner_shard: int32 [2, 4096, 16, 1], P(None, ('grp', 'shard')), may hold values from 0 to 7; in each aligned block of 2048 rows (0 to 2047, 2048 to 4095, ..., all dimensions but the last counted through in order) at most 512 rows name the same one
- local_row: int32 [2, 4096, 16], P(None, ('grp', 'shard')), may hold values from 0 to 511
- click_label: int32 [2, 4096], P(None, ('grp', 'shard')), may hold values 0 or 1
- row_table: float32 [4096, 128], P('shard'), may hold values from -3 to 3
- squared_sums: float32 [4096, 128], P('shard'), may hold values from 0.01 to 1
- w_input: bfloat16 [512, 1024], replicated, may hold values from -0.25 to 0.25
- w_hidden: bfloat16 [1024, 1024], replicated, may hold values from -0.1875 to 0.1875
- w_output: bfloat16 [1024], replicated, may hold values from -0.1875 to 0.1875
Outputs:
- new_table: float32 [4096, 128], P('shard')
- logits: float32 [2, 4096], P(None, ('grp', 'shard'))
- input_grad: float32 [524288], P(('grp', 'shard'))
Inputs may be any that keep to these rules, and one draw needn't show every extreme that they name: `owner_shard`: within the ids of one device in one minibatch (aligned blocks of 2048 ids), at most 512 name the same owner shard, and that many do in some block.
All inputs are finite; a program needn't handle non-finite values. No bound on the sum of `click_label` on one device may be relied on, other than what follows from the above.
Results may differ from a plain program's by a relative error of at most 0.0039.
The roundings to bfloat16 on the way count: a program that leaves them out, or rounds other values in their place, can miss the bound.
Values may be sent and summed in bfloat16 or wider, within the bound.
A program may use at most 64 MiB of HBM per device.

v0:
```python
import jax
import jax.numpy as jnp
from jax import lax
from jax.sharding import PartitionSpec as P

SLOTS = 4
HOT = 4


learn_rate = 0.1


def mlp_pass(rows, labels, w_input, w_hidden, w_output):
    count = rows.shape[0]
    width = rows.shape[2]
    pooled = jnp.sum(rows.reshape(count, SLOTS, HOT, width), axis=2, dtype=jnp.float32)
    pooled = pooled.astype(jnp.bfloat16).reshape(count, SLOTS * width)
    pre_one = jnp.dot(pooled, w_input, preferred_element_type=jnp.float32)
    act_one = jnp.maximum(pre_one, 0.0).astype(jnp.bfloat16)
    pre_two = jnp.dot(act_one, w_hidden, preferred_element_type=jnp.float32)
    act_two = jnp.maximum(pre_two, 0.0).astype(jnp.bfloat16)
    logits = jnp.dot(act_two, w_output, preferred_element_type=jnp.float32)
    slope = jax.nn.sigmoid(logits) - labels
    back_two = jnp.where(
        pre_two > 0, slope[:, None] * w_output.astype(jnp.float32)[None, :], 0.0
    ).astype(jnp.bfloat16)
    back_one = lax.dot_general(
        back_two, w_hidden, (((1,), (1,)), ((), ())), preferred_element_type=jnp.float32
    )
    back_one = jnp.where(pre_one > 0, back_one, 0.0).astype(jnp.bfloat16)
    back_in = lax.dot_general(
        back_one, w_input, (((1,), (1,)), ((), ())), preferred_element_type=jnp.float32
    )
    back_in = back_in.astype(jnp.bfloat16)
    weight_term = lax.dot_general(
        pooled, back_one, (((0,), (0,)), ((), ())), preferred_element_type=jnp.float32
    )
    lookup_grad = jnp.broadcast_to(
        back_in.reshape(count, SLOTS, 1, width), (count, SLOTS, HOT, width)
    )
    return (logits, lookup_grad.reshape(count * SLOTS * HOT, width), weight_term)


def place_slots(owner_ids, shards, capacity):
    batches = owner_ids.shape[0]
    onehot = (owner_ids[:, :, None] == jnp.arange(shards, dtype=jnp.int32)[None, None, :]).astype(
        jnp.int32
    )
    position = jnp.sum((jnp.cumsum(onehot, axis=1) - 1) * onehot, axis=2)
    offsets = jnp.arange(batches, dtype=jnp.int32)[:, None] * capacity
    return owner_ids * (batches * capacity) + offsets + position


def window_pass(owner_ids, row_ids, labels, table_low, w_input, w_hidden, w_output):
    batches, samples, looks = row_ids.shape
    shards = lax.axis_size("shard")
    row_count = table_low.shape[0]
    width = table_low.shape[1]
    capacity = 2 * samples * looks // shards
    flat_owner = owner_ids.reshape(batches, samples * looks)
    flat_row = row_ids.reshape(batches, samples * looks)
    slots = place_slots(flat_owner, shards, capacity).reshape(-1)
    columns = batches * capacity
    request = (
        jnp.zeros((shards * columns,), jnp.int32)
        .at[slots]
        .set(flat_row.reshape(-1))
        .reshape(shards, columns)
    )
    asked = lax.all_to_all(request, "shard", split_axis=0, concat_axis=0, tiled=True)
    served = lax.all_to_all(table_low[asked], "shard", split_axis=0, concat_axis=0, tiled=True)
    looked = served.reshape(shards * columns, width)[slots]
    logits, lookup_grad, weight_term = mlp_pass(
        looked.reshape(batches * samples, looks, width),
        labels.reshape(-1),
        w_input,
        w_hidden,
        w_output,
    )
    outgoing = (
        jnp.zeros((shards * columns, width), jnp.bfloat16)
        .at[slots]
        .set(lookup_grad)
        .reshape(shards, columns, width)
    )
    incoming = lax.all_to_all(outgoing, "shard", split_axis=0, concat_axis=0, tiled=True)
    row_grad = jax.ops.segment_sum(
        incoming.reshape(-1, width).astype(jnp.float32), asked.reshape(-1), num_segments=row_count
    )
    return (logits.reshape(batches, samples), row_grad, weight_term)


def adagrad_step(table_part, sums_part, grad_part):
    new_sums = sums_part + grad_part * grad_part
    return table_part - learn_rate * grad_part / jnp.sqrt(new_sums)


def local(
    owner_shard, local_row, click_label, row_table, squared_sums, w_input, w_hidden, w_output
):
    table_low = row_table.astype(jnp.bfloat16)
    owner_ids = owner_shard[..., 0]
    labels = click_label.astype(jnp.float32)
    logit_parts = []
    row_grad = jnp.zeros(row_table.shape, jnp.float32)
    weight_sum = jnp.zeros(w_input.shape, jnp.float32)
    for batch in range(local_row.shape[0]):
        part_logits, part_grad, part_weight = window_pass(
            owner_ids[batch : batch + 1],
            local_row[batch : batch + 1],
            labels[batch : batch + 1],
            table_low,
            w_input,
            w_hidden,
            w_output,
        )
        logit_parts.append(part_logits)
        row_grad = row_grad + part_grad
        weight_sum = weight_sum + part_weight
    logits = jnp.concatenate(logit_parts, axis=0)
    input_grad = lax.psum_scatter(
        weight_sum.reshape(-1), ("grp", "shard"), scatter_dimension=0, tiled=True
    )
    total = lax.psum(row_grad.astype(jnp.bfloat16), "grp").astype(jnp.float32)
    new_table = adagrad_step(row_table, squared_sums, total)
    return (new_table, logits, input_grad)


def solution(mesh):
    in_specs = (
        P(None, ("grp", "shard"), None, None),
        P(None, ("grp", "shard"), None),
        P(None, ("grp", "shard")),
        P("shard", None),
        P("shard", None),
        P(),
        P(),
        P(),
    )
    out_specs = (P("shard", None), P(None, ("grp", "shard")), P(("grp", "shard")))
    return jax.shard_map(local, mesh=mesh, in_specs=in_specs, out_specs=out_specs, check_vma=False)
```

profile of v0, /device:TPU:0, one launch (start us, length us, event | category | flops | bytes accessed | tf_op | source)
XLA Modules:
  0.0 332.8 jit_solution(12489809370181049437)
XLA Ops:
  7.2 0.9 fusion.60
  8.3 2.3 reduce-window.14
  11.4 0.7 fusion.59
  12.4 8.6 %scatter_custom_fusion = s32[4096]{0:T(1024)} fusion(s32[2048]{0:T(1024)S(1)} %bitcast.157, s32[2048]{0:T(1024)S(1)} %reshape.501, s32[]{:T(128)} %constant.10.clone.1), kind=kCustom, calls=%fused_computation.89 | custom fusion | bytes 16388 | tf_op jit(solution)/shard_map/scatter | solution.py:67
  21.0 5.2 %all-to-all-start = ((s32[8,1,512]{2,1,0:T(1,128)}), s32[8,1,512]{2,1,0:T(1,128)S(1)}, u32[]{:S(2)}, u32[]{:S(2)}) async-start(s32[8,1,512]{2,1,0:T(1,128)} %bitcast.6), calls=%async_computation | async-start | bytes 32768 | tf_op jit(solution)/shard_map/all_to_all | solution.py:70
  26.4 2.3 reduce-window.16
  29.8 8.6 %scatter_custom_fusion.3 = s32[4096]{0:T(1024)} fusion(s32[2048]{0:T(1024)S(1)} %bitcast.160, s32[2048]{0:T(1024)S(1)} %reshape.525, s32[]{:T(128)} %constant.10.clone.1), kind=kCustom, calls=%fused_computation.87 | custom fusion | bytes 16388 | tf_op jit(solution)/shard_map/scatter | solution.py:67
  38.4 4.2 %all-to-all-start.3 = ((s32[8,1,512]{2,1,0:T(1,128)}), s32[8,1,512]{2,1,0:T(1,128)S(1)}, u32[]{:S(2)}, u32[]{:S(2)}) async-start(s32[8,1,512]{2,1,0:T(1,128)} %bitcast.24), calls=%async_computation.3 | async-start | bytes 32768 | tf_op jit(solution)/shard_map/all_to_all | solution.py:70
  42.7 14.9 %gather_fusion = bf16[4096,128]{1,0:T(8,128)(2,1)} fusion(bf16[512,128]{1,0:T(8,128)(2,1)S(1)} %convert_element_type.80, s32[4096]{0:T(1024)S(1)} %broadcast_clamp_fusion.1), kind=kCustom, calls=%fused_computation | custom fusion | bytes 2113536 | tf_op jit(solution)/shard_map/gather | solution.py:71
  57.6 4.2 %all-to-all-start.1 = ((bf16[8,512,128]{2,1,0:T(8,128)(2,1)}), bf16[8,512,128]{2,1,0:T(8,128)(2,1)S(1)}, u32[]{:S(2)}, u32[]{:S(2)}) async-start(bf16[8,512,128]{2,1,0:T(8,128)(2,1)} %bitcast.142), calls=%async_computation.1 | async-start | bytes 2097152 | tf_op jit(solution)/shard_map/all_to_all | solution.py:71
  61.8 14.9 %gather_fusion.2 = bf16[4096,128]{1,0:T(8,128)(2,1)} fusion(bf16[512,128]{1,0:T(8,128)(2,1)S(1)} %convert_element_type.80, s32[4096]{0:T(1024)S(1)} %broadcast_clamp_fusion), kind=kCustom, calls=%fused_computation.2 | custom fusion | bytes 2113536 | tf_op jit(solution)/shard_map/gather | solution.py:71
  76.7 0.5 all-to-all-done.1
  77.2 4.2 %all-to-all-start.4 = ((bf16[8,512,128]{2,1,0:T(8,128)(2,1)}), bf16[8,512,128]{2,1,0:T(8,128)(2,1)}, u32[]{:S(2)}, u32[]{:S(2)}) async-start(bf16[8,512,128]{2,1,0:T(8,128)(2,1)} %bitcast.141), calls=%async_computation.4 | async-start | bytes 2097152 | tf_op jit(solution)/shard_map/all_to_all | solution.py:71
  81.4 0.6 convert_element_type.84
  82.1 8.0 %gather_fusion.1 = bf16[2048,128]{1,0:T(8,128)(2,1)} fusion(bf16[4096,128]{1,0:T(8,128)(2,1)S(1)} %bitcast.139, s32[2048]{0:T(1024)S(1)} %broadcast_clamp_fusion.3), kind=kCustom, calls=%fused_computation.1 | custom fusion | bytes 1056768 | tf_op jit(solution)/shard_map/gather | solution.py:72
  90.0 1.7 reduce_sum.48
  91.8 5.0 %all-to-all-done.4 = bf16[8,512,128]{2,1,0:T(8,128)(2,1)} async-done(((bf16[8,512,128]{2,1,0:T(8,128)(2,1)}), bf16[8,512,128]{2,1,0:T(8,128)(2,1)}, u32[]{:S(2)}, u32[]{:S(2)}) %all-to-all-start.4) | async-done | bytes 1048608 | tf_op jit(solution)/shard_map/all_to_all | solution.py:71
  96.8 9.1 %gather_fusion.3 = bf16[2048,128]{1,0:T(8,128)(2,1)} fusion(bf16[4096,128]{1,0:T(8,128)(2,1)} %bitcast.29, s32[2048]{0:T(1024)S(1)} %broadcast_clamp_fusion.2), kind=kCustom, calls=%fused_computation.3 | custom fusion | bytes 1056768 | tf_op jit(solution)/shard_map/gather | solution.py:72
  105.9 1.7 reduce_sum.51
  108.0 0.3 fusion.29
  108.3 0.5 fusion.14
  108.8 0.4 fusion.16
  109.4 0.6 copy-done.3
  110.1 0.7 divide_subtract_fusion
  110.8 0.8 fusion.4
  111.6 1.1 convolution_convert_fusion.1
  112.8 1.6 broadcast_in_dim.13
  114.4 1.9 broadcast_in_dim.14
  116.2 7.1 %scatter_custom_fusion.1 = bf16[4096,128]{1,0:T(8,128)(2,1)} fusion(s32[2048]{0:T(1024)} %bitcast.159, bf16[2048,128]{1,0:T(8,128)(2,1)} %bitcast.152, bf16[]{:T(256)} %constant.14.clone.1), kind=kCustom, calls=%fused_computation.29 | custom fusion | bytes 1049088 | tf_op jit(solution)/shard_map/scatter | solution.py:83
  123.4 4.4 %all-to-all-start.2 = ((bf16[8,512,128]{2,1,0:T(8,128)(2,1)}), bf16[8,512,128]{2,1,0:T(8,128)(2,1)}, u32[]{:S(2)}, u32[]{:S(2)}) async-start(bf16[8,512,128]{2,1,0:T(8,128)(2,1)} %bitcast.144), calls=%async_computation.2 | async-start | bytes 2097152 | tf_op jit(solution)/shard_map/all_to_all | solution.py:86
  127.8 2.1 fusion.5
  129.9 0.7 copy-done.4
  130.6 1.1 convolution_convert_fusion
  131.7 0.9 broadcast_in_dim.15
  132.8 7.0 %scatter_custom_fusion.4 = bf16[4096,128]{1,0:T(8,128)(2,1)} fusion(s32[2048]{0:T(1024)} %bitcast.162, bf16[2048,128]{1,0:T(8,128)(2,1)S(1)} %bitcast.151, bf16[]{:T(256)} %constant.14.clone.1), kind=kCustom, calls=%fused_computation.27 | custom fusion | bytes 1049088 | tf_op jit(solution)/shard_map/scatter | solution.py:83
  139.8 2.7 fusion.31
  142.5 0.5 all-to-all-done.2
  143.1 3.6 %all-to-all-start.5 = ((bf16[8,512,128]{2,1,0:T(8,128)(2,1)}), bf16[8,512,128]{2,1,0:T(8,128)(2,1)S(1)}, u32[]{:S(2)}, u32[]{:S(2)}) async-start(bf16[8,512,128]{2,1,0:T(8,128)(2,1)} %bitcast.34), calls=%async_computation.5 | async-start | bytes 2097152 | tf_op jit(solution)/shard_map/all_to_all | solution.py:86
  146.7 2.0 add_bitcast_fusion
  148.7 1.8 copy.33
  150.6 23.4 %scatter_custom_fusion.2 = f32[512,128]{1,0:T(8,128)} fusion(s32[4096]{0:T(1024)S(1)} %bitcast.153, bf16[4096,128]{1,0:T(8,128)(2,1)} %bitcast.36, f32[]{:T(128)} %constant.9.clone.1), kind=kCustom, calls=%fused_computation.12 | custom fusion | flops 1048576 | bytes 1310724 | tf_op jit(solution)/shard_map/scatter-add | solution.py:87
  174.0 23.2 %scatter_custom_fusion.5 = f32[512,128]{1,0:T(8,128)} fusion(s32[4096]{0:T(1024)} %bitcast.154, bf16[4096,128]{1,0:T(8,128)(2,1)S(1)} %bitcast.143, f32[]{:T(128)} %constant.9.clone.1), kind=kCustom, calls=%fused_computation.10 | custom fusion | flops 1048576 | bytes 1311232 | tf_op jit(solution)/shard_map/scatter-add | solution.py:87
  197.2 1.7 add_convert_fusion
  199.0 0.6 pad_maximum_fusion
  199.5 88.8 %all-reduce.6.cloned.1.call-done = f32[524288]{0:T(1024)} async-done(((f32[524288]{0:T(1024)}), f32[524288]{0:T(1024)}) %all-reduce.6.cloned.1.call-update) | async-done | bytes 2097168
  288.4 1.5 dynamic-slice
  289.8 34.3 %all-reduce.4.cloned.1.call-done = bf16[512,128]{1,0:T(8,128)(2,1)} async-done(((bf16[512,128]{1,0:T(8,128)(2,1)}), bf16[512,128]{1,0:T(8,128)(2,1)}) %all-reduce.4.cloned.1.call-update) | async-done | bytes 131088 | tf_op jit(solution)/shard_map/psum | solution.py:124
  324.2 1.8 fusion.11
  (83 shorter events, 3.4 us)
Async XLA Ops:
  7.2 101.1 %copy-start = (bf16[1024,1024]{1,0:T(8,128)(2,1)S(1)}, bf16[1024,1024]{1,0:T(8,128)(2,1)}, u32[]{:S(2)}) copy-start(bf16[1024,1024]{1,0:T(8,128)(2,1)} %param.14) | copy-start | bytes 6291460
  7.2 22.4 %copy-start.7 = (f32[512,128]{1,0:T(8,128)S(1)}, f32[512,128]{1,0:T(8,128)}, u32[]{:S(2)}) copy-start(f32[512,128]{1,0:T(8,128)} %param.11) | copy-start | bytes 786436
  12.4 69.7 %copy-start.11 = (s32[2048,1]{0,1:T(1,128)}, s32[2048,1]{0,1:T(1,128)S(1)}, u32[]{:S(2)}) copy-start(s32[2048,1]{0,1:T(1,128)S(1)} %compare_select_fusion.3) | copy-start | bytes 24580
  21.0 17.4 %all-to-all-start = ((s32[8,1,512]{2,1,0:T(1,128)}), s32[8,1,512]{2,1,0:T(1,128)S(1)}, u32[]{:S(2)}, u32[]{:S(2)}) async-start(s32[8,1,512]{2,1,0:T(1,128)} %bitcast.6), calls=%async_computation | async-start | bytes 32768 | tf_op jit(solution)/shard_map/all_to_all | solution.py:70
  29.6 52.5 %copy-start.12 = (s32[2048,1]{0,1:T(1,128)}, s32[2048,1]{0,1:T(1,128)S(1)}, u32[]{:S(2)}) copy-start(s32[2048,1]{0,1:T(1,128)S(1)} %compare_select_fusion.2) | copy-start | bytes 24580
  38.4 19.1 %all-to-all-start.3 = ((s32[8,1,512]{2,1,0:T(1,128)}), s32[8,1,512]{2,1,0:T(1,128)S(1)}, u32[]{:S(2)}, u32[]{:S(2)}) async-start(s32[8,1,512]{2,1,0:T(1,128)} %bitcast.24), calls=%async_computation.3 | async-start | bytes 32768 | tf_op jit(solution)/shard_map/all_to_all | solution.py:70
  57.6 4.2 %copy-start.9 = (s32[8,1,512]{2,1,0:T(1,128)}, s32[8,1,512]{2,1,0:T(1,128)S(1)}, u32[]{:S(2)}) copy-start(s32[8,1,512]{2,1,0:T(1,128)S(1)} %all-to-all-done.3) | copy-start | bytes 49156
  57.6 19.6 %all-to-all-start.1 = ((bf16[8,512,128]{2,1,0:T(8,128)(2,1)}), bf16[8,512,128]{2,1,0:T(8,128)(2,1)S(1)}, u32[]{:S(2)}, u32[]{:S(2)}) async-start(bf16[8,512,128]{2,1,0:T(8,128)(2,1)} %bitcast.142), calls=%async_computation.1 | async-start | bytes 2097152 | tf_op jit(solution)/shard_map/all_to_all | solution.py:71
  76.7 4.7 %copy-start.13 = (bf16[1024]{0:T(1024)(128)(2,1)S(1)}, bf16[1024]{0:T(1024)(128)(2,1)}, u32[]{:S(2)}) copy-start(bf16[1024]{0:T(1024)(128)(2,1)} %param.15) | copy-start | bytes 6148
  76.7 5.3 %copy-start.17 = (s32[2,128]{1,0:T(2,128)S(1)}, s32[2,128]{1,0:T(2,128)}, u32[]{:S(2)}) copy-start(s32[2,128]{1,0:T(2,128)} %param.10) | copy-start | bytes 3076
  77.2 19.7 %all-to-all-start.4 = ((bf16[8,512,128]{2,1,0:T(8,128)(2,1)}), bf16[8,512,128]{2,1,0:T(8,128)(2,1)}, u32[]{:S(2)}, u32[]{:S(2)}) async-start(bf16[8,512,128]{2,1,0:T(8,128)(2,1)} %bitcast.141), calls=%async_computation.4 | async-start | bytes 2097152 | tf_op jit(solution)/shard_map/all_to_all | solution.py:71
  91.8 15.9 %copy-start.6 = (bf16[128,4,128]{2,1,0:T(4,128)(2,1)}, bf16[128,4,128]{2,1,0:T(4,128)(2,1)S(1)}, u32[]{:S(2)}) copy-start(bf16[128,4,128]{2,1,0:T(4,128)(2,1)S(1)} %reduce_sum.48) | copy-start | bytes 393220
  96.8 10.8 %copy-start.1 = (bf16[512,1024]{1,0:T(8,128)(2,1)S(1)}, bf16[512,1024]{1,0:T(8,128)(2,1)}, u32[]{:S(2)}) copy-start(bf16[512,1024]{1,0:T(8,128)(2,1)} %param.13) | copy-start | bytes 3145732
  108.3 0.9 copy-start.2
  108.8 2.0 copy-start.10
  109.3 0.8 copy-start.3
  110.1 0.7 copy-start.14
  123.4 19.7 %all-to-all-start.2 = ((bf16[8,512,128]{2,1,0:T(8,128)(2,1)}), bf16[8,512,128]{2,1,0:T(8,128)(2,1)}, u32[]{:S(2)}, u32[]{:S(2)}) async-start(bf16[8,512,128]{2,1,0:T(8,128)(2,1)} %bitcast.144), calls=%async_computation.2 | async-start | bytes 2097152 | tf_op jit(solution)/shard_map/all_to_all | solution.py:86
  129.9 0.7 copy-start.4
  142.5 4.1 %copy-start.5 = (bf16[128,1024]{1,0:T(8,128)(2,1)S(1)}, bf16[128,1024]{1,0:T(8,128)(2,1)}, u32[]{:S(2)}) copy-start(bf16[128,1024]{1,0:T(8,128)(2,1)} %copy-done.4) | copy-start | bytes 786436
  143.1 31.0 %all-to-all-start.5 = ((bf16[8,512,128]{2,1,0:T(8,128)(2,1)}), bf16[8,512,128]{2,1,0:T(8,128)(2,1)S(1)}, u32[]{:S(2)}, u32[]{:S(2)}) async-start(bf16[8,512,128]{2,1,0:T(8,128)(2,1)} %bitcast.34), calls=%async_computation.5 | async-start | bytes 2097152 | tf_op jit(solution)/shard_map/all_to_all | solution.py:86
  146.6 141.8 %all-reduce.6.cloned.1.call-start = ((), (), s32[]{:S(2)}) async-start(), calls=%async_computation.7 | async-start | bytes 4194304
  150.5 48.4 %copy-start.15 = (f32[1,128]{1,0:T(1,128)S(1)}, f32[1,128]{1,0:T(1,128)}, u32[]{:S(2)}) copy-start(f32[1,128]{1,0:T(1,128)} %copy-done.14) | copy-start | bytes 1540
  150.5 48.4 %copy-start.16 = (f32[1,128]{1,0:T(1,128)S(1)}, f32[1,128]{1,0:T(1,128)}, u32[]{:S(2)}) copy-start(f32[1,128]{1,0:T(1,128)} %get-tuple-element.11) | copy-start | bytes 1540
  150.5 173.7 %copy-start.8 = (f32[512,128]{1,0:T(8,128)S(1)}, f32[512,128]{1,0:T(8,128)}, u32[]{:S(2)}) copy-start(f32[512,128]{1,0:T(8,128)} %param.11) | copy-start | bytes 786436
  150.5 173.6 %all-reduce.4.cloned.1.call-start = ((), (), s32[]{:S(2)}) async-start(), calls=%async_computation.6 | async-start | bytes 262144 | tf_op jit(solution)/shard_map/psum | solution.py:124
Sparse Core Ops, SparseCore 0:
  152.8 135.5 all-reduce.5
  290.8 33.3 all-reduce.3
where the time goes:
time: 334 us; the launch traced here: 333 us
  waiting for transfers between devices  129 us (39%)
  local copies, waits for them, and re-layouts  90 us (27%)
  other arithmetic  60.8 us (18%)
  starting transfers between devices  25.9 us (8%)
  between operations  14.5 us (4%)
  matrix products  12.3 us (4%)
    unnamed x3, waiting for transfers between devices  88.9 us
    scatter-add x2, other arithmetic, window_pass(): jax.ops.segment_sum(incoming.reshape(-1, width).astype(jnp.float32), aske...  46.6 us
    psum x1, waiting for transfers between devices, local(): total = lax.psum(row_grad.astype(jnp.bfloat16), 'grp').astype(jnp.float32)  34.3 us
    gather x2, local copies, waits for them, and re-layouts, window_pass(): table_low[asked]  29.8 us
    scatter x2, local copies, waits for them, and re-layouts, window_pass(): request = jnp.zeros((shards * columns,), jnp.int32).at[slots].set(flat_ro...  17.2 us
    gather x2, local copies, waits for them, and re-layouts, window_pass(): looked = served.reshape(shards * columns, width)[slots]  17.1 us
    scatter x2, local copies, waits for them, and re-layouts, window_pass(): outgoing = jnp.zeros((shards * columns, width), jnp.bfloat16).at[slots].s...  14.1 us
    all_to_all x2, starting transfers between devices, window_pass(): lax.all_to_all(request, 'shard', split_axis=0, concat_axis=0, tiled=True)  9.37 us
  transfers between devices with their start and end apart: 8, of which 5 were waited for; matrix products, arithmetic and copies ran while one was open for 36% of the time, Pallas kernels for 0%

commit v1 on v0

v1 whole, which is shorter than its diff:
```python
import jax
import jax.numpy as jnp
from jax import lax
from jax.sharding import PartitionSpec as P

SLOTS = 4
HOT = 4


learn_rate = 0.1


def mlp_pass(pooled, labels, w_input, w_hidden, w_output):
    pre_one = jnp.dot(pooled, w_input, preferred_element_type=jnp.float32)
    act_one = jnp.maximum(pre_one, 0.0).astype(jnp.bfloat16)
    pre_two = jnp.dot(act_one, w_hidden, preferred_element_type=jnp.float32)
    act_two = jnp.maximum(pre_two, 0.0).astype(jnp.bfloat16)
    logits = jnp.dot(act_two, w_output, preferred_element_type=jnp.float32)
    slope = jax.nn.sigmoid(logits) - labels
    back_two = jnp.where(
        pre_two > 0, slope[:, None] * w_output.astype(jnp.float32)[None, :], 0.0
    ).astype(jnp.bfloat16)
    back_one = lax.dot_general(
        back_two, w_hidden, (((1,), (1,)), ((), ())), preferred_element_type=jnp.float32
    )
    back_one = jnp.where(pre_one > 0, back_one, 0.0).astype(jnp.bfloat16)
    back_in = lax.dot_general(
        back_one, w_input, (((1,), (1,)), ((), ())), preferred_element_type=jnp.float32
    )
    back_in = back_in.astype(jnp.bfloat16)
    weight_term = lax.dot_general(
        pooled, back_one, (((0,), (0,)), ((), ())), preferred_element_type=jnp.float32
    )
    return (logits, back_in, weight_term)


def adagrad_step(table_part, sums_part, grad_part):
    new_sums = sums_part + grad_part * grad_part
    return table_part - learn_rate * grad_part / jnp.sqrt(new_sums)


def local(
    owner_shard, local_row, click_label, row_table, squared_sums, w_input, w_hidden, w_output
):
    row_count, width = row_table.shape
    batches, samples, looks = local_row.shape
    table_all = lax.all_gather(row_table.astype(jnp.bfloat16), "shard", axis=0, tiled=True)
    ids = (owner_shard[..., 0] * row_count + local_row).reshape(-1, HOT)
    rows = jnp.arange(table_all.shape[0], dtype=jnp.int32)
    counts = jnp.sum(
        (ids[:, :, None] == rows[None, None, :]).astype(jnp.float32), axis=1
    ).astype(jnp.bfloat16)
    pooled = jnp.dot(counts, table_all, preferred_element_type=jnp.float32)
    pooled = pooled.astype(jnp.bfloat16).reshape(batches * samples, SLOTS * width)
    labels = click_label.astype(jnp.float32).reshape(-1)
    logits, back_in, weight_term = mlp_pass(pooled, labels, w_input, w_hidden, w_output)
    row_part = lax.dot_general(
        counts,
        back_in.reshape(-1, width),
        (((0,), (0,)), ((), ())),
        preferred_element_type=jnp.float32,
    )
    row_grad = lax.psum_scatter(row_part, "shard", scatter_dimension=0, tiled=True)
    total = lax.psum(row_grad.astype(jnp.bfloat16), "grp").astype(jnp.float32)
    input_grad = lax.psum_scatter(
        weight_term.reshape(-1), ("grp", "shard"), scatter_dimension=0, tiled=True
    )
    new_table = adagrad_step(row_table, squared_sums, total)
    return (new_table, logits.reshape(batches, samples), input_grad)


def solution(mesh):
    in_specs = (
        P(None, ("grp", "shard"), None, None),
        P(None, ("grp", "shard"), None),
        P(None, ("grp", "shard")),
        P("shard", None),
        P("shard", None),
        P(),
        P(),
        P(),
    )
    out_specs = (P("shard", None), P(None, ("grp", "shard")), P(("grp", "shard")))
    return jax.shard_map(local, mesh=mesh, in_specs=in_specs, out_specs=out_specs, check_vma=False)
```

time: 334 us -> 283 us (0.85)
  waiting for transfers between devices: 129 us -> 219 us
  local copies, waits for them, and re-layouts: 90 us -> 8.42 us
  other arithmetic: 60.8 us -> 23.7 us
  starting transfers between devices: 25.9 us -> 0.16 us
  matrix products: 12.3 us -> 17.6 us
    unnamed x3 -> x5, waiting for transfers between devices: 88.9 us -> 138 us
    gather x4 -> x0, local copies, waits for them, and re-layouts: 46.8 us -> none  [the longest x2 29.8 us: window_pass(): table_low[asked]]
    scatter-add x2 -> x0, other arithmetic: 46.6 us -> none  [window_pass(): jax.ops.segment_sum(incoming.reshape(-1, width).astype(jnp.float32), aske...]
    reduce_scatter x0 -> x1, waiting for transfers between devices: none -> 38.1 us  [local(): lax.psum_scatter(row_part, 'shard', scatter_dimension=0, tiled=True)]
    scatter x4 -> x0, local copies, waits for them, and re-layouts: 31.4 us -> none  [the longest x2 17.2 us: window_pass(): request = jnp.zeros((shards * columns,), jnp.int32).at[slots].set(flat_ro...]
    all_to_all x6 -> x0, starting transfers between devices: 25.8 us -> none  [the longest x2 9.37 us: window_pass(): lax.all_to_all(request, 'shard', split_axis=0, concat_axis=0, tiled=True)]
    dot_general x0 -> x2, matrix products: none -> 13.8 us  [the longest x1 7.13 us: local(): lax.dot_general(counts, back_in.reshape(-1, width), (((0,), (0,)), ((), (...]
    reduce_sum x4 -> x1, other arithmetic: 3.66 us -> 17.2 us  [local(): jnp.sum((ids[:, :, None] == rows[None, None, :]).astype(jnp.float32), axi...]
  transfers between devices with their start and end apart: 8 -> 4, of which waited for: 5 -> 4; matrix products, arithmetic and copies ran while one was open for 36% -> 9% of each run, Pallas kernels for 0% -> 0%
where the time goes in v1:
time: 283 us
  waiting for transfers between devices  219 us (77%)
  other arithmetic  23.7 us (8%)
  matrix products  17.6 us (6%)
  between operations  13.9 us (5%)
  local copies, waits for them, and re-layouts  8.42 us (3%)
    unnamed x5, waiting for transfers between devices  138 us
    reduce_scatter x1, waiting for transfers between devices, local(): lax.psum_scatter(row_part, 'shard', scatter_dimension=0, tiled=True)  38.1 us
    psum x1, waiting for transfers between devices, local(): total = lax.psum(row_grad.astype(jnp.bfloat16), 'grp').astype(jnp.float32)  34.7 us
    reduce_sum x1, other arithmetic, local(): jnp.sum((ids[:, :, None] == rows[None, None, :]).astype(jnp.float32), axi...  17.2 us
    all_gather x1, waiting for transfers between devices, local(): lax.all_gather(row_table.astype(jnp.bfloat16), 'shard', axis=0, tiled=True)  7.89 us
    dot_general x1, matrix products, local(): lax.dot_general(counts, back_in.reshape(-1, width), (((0,), (0,)), ((), (...  7.13 us
    dot_general x1, matrix products, local(): pooled = jnp.dot(counts, table_all, preferred_element_type=jnp.float32)  6.64 us
    unnamed x19, local copies, waits for them, and re-layouts  5.74 us
  transfers between devices with their start and end apart: 4, of which 4 were waited for; matrix products, arithmetic and copies ran while one was open for 9% of the time, Pallas kernels for 0%

profile of v1, /device:TPU:0, one launch (start us, length us, event | category | flops | bytes accessed | tf_op | source)
XLA Modules:
  0.0 282.9 jit_solution(6985868572399818167)
XLA Ops:
  7.2 0.0 copy-start
  7.2 0.0 all-gather.2.cloned.1.call-start
  7.2 1.8 convert_element_type.41
  9.0 0.0 all-gather.2.cloned.1.call-update
  9.0 0.0 reduce-scatter.2.cloned.1.call-start
  9.1 0.7 convert_element_type.46
  9.7 0.7 reshape.31
  10.4 0.7 bitcast_add_fusion
  11.2 0.1 copy.17
  11.3 0.2 eq.15
  11.5 0.2 copy.18
  11.6 17.2 %convert_reduce_fusion = bf16[1024,4096]{1,0:T(8,128)(2,1)} fusion(s32[1024,4]{0,1:T(4,128)S(1)} %copy.18), kind=kLoop, calls=%fused_computation | loop fusion | flops 46137344 | bytes 8404992 | tf_op jit(solution)/shard_map/reduce_sum | solution.py:50
  28.8 0.0 copy-start.1
  28.8 7.9 %all-gather.2.cloned.1.call-done = bf16[4096,128]{1,0:T(8,128)(2,1)} async-done(((bf16[512,128]{1,0:T(8,128)(2,1)}), bf16[4096,128]{1,0:T(8,128)(2,1)}) %all-gather.2.cloned.1.call-update) | async-done | bytes 1048592 | tf_op jit(solution)/shard_map/all_gather | solution.py:47
  36.7 6.6 %fusion.5 = bf16[1024,128]{1,0:T(8,128)(2,1)} fusion(bf16[4096,128]{1,0:T(8,128)(2,1)} %all-gather.2.cloned.1.call-done, bf16[1024,4096]{1,0:T(8,128)(2,1)} %convert_reduce_fusion), kind=kOutput, calls=%fused_computation.9 | convolution fusion | flops 1073872896 | bytes 9699328 | tf_op jit(solution)/shard_map/dot_general | solution.py:53
  43.4 1.1 reshape.26
  44.5 0.0 copy-done.1
  44.5 0.4 fusion.22
  44.9 0.0 copy-done
  44.9 0.0 copy-start.7
  45.0 0.7 fusion.8
  45.7 0.2 fusion.9
  45.9 0.0 copy-start.6
  45.9 0.0 copy-done.7
  46.0 0.8 fusion.4
  46.8 0.0 copy-done.6
  46.8 0.0 copy-start.2
  46.8 0.8 copy-done.2
  47.6 1.2 convolution_convert_fusion
  48.8 1.1 reshape.28
  49.9 7.1 %fusion.23 = f32[4096,128]{1,0:T(8,128)} fusion(bf16[1024,4096]{1,0:T(8,128)(2,1)} %convert_reduce_fusion, bf16[1024,128]{1,0:T(8,128)(2,1)S(1)} %reshape.28), kind=kOutput, calls=%fused_computation.33 | convolution fusion | flops 1073741824 | bytes 10747904 | tf_op jit(solution)/shard_map/dot_general | solution.py:57
  57.1 0.0 copy-start.3
  57.1 0.0 reduce-scatter.2.cloned.1.call-update
  57.1 0.0 all-reduce.6.cloned.1.call-start
  57.1 1.0 copy-done.3
  58.1 0.5 convolution_bitcast_fusion
  58.6 1.8 copy.19
  60.3 0.0 all-reduce.6.cloned.1.call-update
  60.4 0.0 all-reduce.4.cloned.1.call-start
  60.4 38.1 %reduce-scatter.2.cloned.1.call-done = f32[512,128]{1,0:T(8,128)} async-done(((f32[4096,128]{1,0:T(8,128)}), f32[512,128]{1,0:T(8,128)}) %reduce-scatter.2.cloned.1.call-update) | async-done | bytes 262160 | tf_op jit(solution)/shard_map/reduce_scatter | solution.py:63
  98.5 1.6 convert_element_type.50
  100.1 0.0 all-reduce.4.cloned.1.call-update
  100.1 138.4 %all-reduce.6.cloned.1.call-done = f32[524288]{0:T(1024)} async-done(((f32[524288]{0:T(1024)}), f32[524288]{0:T(1024)}) %all-reduce.6.cloned.1.call-update) | async-done | bytes 2097168
  238.5 1.5 dynamic-slice
  240.0 34.7 %all-reduce.4.cloned.1.call-done = bf16[512,128]{1,0:T(8,128)(2,1)} async-done(((bf16[512,128]{1,0:T(8,128)(2,1)}), bf16[512,128]{1,0:T(8,128)(2,1)}) %all-reduce.4.cloned.1.call-update) | async-done | bytes 131088 | tf_op jit(solution)/shard_map/psum | solution.py:64
  274.7 0.0 copy-done.4
  274.7 0.0 copy-done.5
  274.7 1.7 fusion.16
  (3 shorter events, 0.0 us)
Async XLA Ops:
  7.2 37.8 %copy-start = (bf16[1024,1024]{1,0:T(8,128)(2,1)S(1)}, bf16[1024,1024]{1,0:T(8,128)(2,1)}, u32[]{:S(2)}) copy-start(bf16[1024,1024]{1,0:T(8,128)(2,1)} %param.14) | copy-start | bytes 6291460
  7.2 29.5 %all-gather.2.cloned.1.call-start = ((), (), s32[]{:S(2)}) async-start(), calls=%async_computation.1 | async-start | bytes 1179648 | tf_op jit(solution)/shard_map/all_gather | solution.py:47
  9.0 89.5 %reduce-scatter.2.cloned.1.call-start = ((), (), s32[]{:S(2)}) async-start(), calls=%async_computation.2 | async-start | bytes 2359296 | tf_op jit(solution)/shard_map/reduce_scatter | solution.py:63
  28.8 15.6 %copy-start.1 = (bf16[512,1024]{1,0:T(8,128)(2,1)S(1)}, bf16[512,1024]{1,0:T(8,128)(2,1)}, u32[]{:S(2)}) copy-start(bf16[512,1024]{1,0:T(8,128)(2,1)} %param.13) | copy-start | bytes 3145732
  44.9 1.0 copy-start.7
  45.9 0.9 copy-start.6
  46.8 0.8 copy-start.2
  57.1 1.0 copy-start.3
  57.1 181.4 %all-reduce.6.cloned.1.call-start = ((), (), s32[]{:S(2)}) async-start(), calls=%async_computation.4 | async-start | bytes 4194304
  60.3 214.3 %copy-start.4 = (f32[512,128]{1,0:T(8,128)S(1)}, f32[512,128]{1,0:T(8,128)}, u32[]{:S(2)}) copy-start(f32[512,128]{1,0:T(8,128)} %param.11) | copy-start | bytes 786436
  60.3 214.3 %copy-start.5 = (f32[512,128]{1,0:T(8,128)S(1)}, f32[512,128]{1,0:T(8,128)}, u32[]{:S(2)}) copy-start(f32[512,128]{1,0:T(8,128)} %param.12) | copy-start | bytes 786436
  60.4 214.3 %all-reduce.4.cloned.1.call-start = ((), (), s32[]{:S(2)}) async-start(), calls=%async_computation.3 | async-start | bytes 262144 | tf_op jit(solution)/shard_map/psum | solution.py:64
Sparse Core Ops, SparseCore 0:
  10.5 26.1 all-gather.1
  57.2 41.2 reduce-scatter.1
  104.7 133.8 all-reduce.5
  241.3 33.3 all-reduce.3

commit v2 on v1

v2 whole, which is shorter than its diff:
```python
import functools

import jax
import jax.numpy as jnp
from jax import lax
from jax.experimental import pallas as pl
from jax.experimental.pallas import tpu as pltpu
from jax.sharding import PartitionSpec as P

SLOTS = 4
HOT = 4
HALVES = 2
TILE = 256
MESH = pl.DeviceIdType.MESH

learn_rate = 0.1


def flip(index, mask):
    bit = 1
    while bit <= mask:
        if mask & bit:
            index = index + bit - 2 * bit * lax.rem(lax.div(index, bit), 2)
        bit *= 2
    return index


def bits_of(count):
    return [1 << i for i in range(count.bit_length() - 1)]


def high_first(order, place):
    relative = {"shard": 0, "grp": 0}
    for i, (axis, bit) in enumerate(order):
        if place >> (len(order) - 1 - i) & 1:
            relative[axis] |= bit
    return relative


def low_first(order, place):
    return high_first(order[::-1], place)


def kernel(
    n_shard,
    n_grp,
    keep,
    scatter,
    owner_ref,
    row_ref,
    label_ref,
    table_ref,
    sums_ref,
    w_in_hbm,
    w_hid_hbm,
    w_out_ref,
    new_ref,
    logit_ref,
    weight_ref,
    w_in,
    w_hid,
    gathered,
    keys,
    counts,
    lookups,
    pooled,
    pre_one,
    act_one,
    pre_two,
    act_two,
    back_two,
    back_one,
    row_sum,
    row_out,
    row_in,
    weight_term,
    weight_sum,
    weight_out,
    weight_in,
    load_sem,
    gather_send,
    gather_recv,
    row_send,
    row_recv,
    weight_send,
    weight_recv,
):
    samples = owner_ref.shape[0]
    rows, width = table_ref.shape
    hidden = w_hid.shape[0]
    half = rows // HALVES
    me = {"shard": lax.axis_index("shard"), "grp": lax.axis_index("grp")}
    shard_bits = [("shard", b) for b in bits_of(n_shard)]
    grp_bits = [("grp", b) for b in bits_of(n_grp)]
    near, far = shard_bits[:1], shard_bits[1:]
    gather_order = [far[::-1] + near, far + near]
    row_order = near + far
    weight_order = near + far[::-1] + grp_bits[::-1]

    def partner(step):
        axis, bit = step
        return {axis: flip(me[axis], bit)}

    load_in = pltpu.make_async_copy(w_in_hbm, w_in, load_sem.at[0])
    load_hid = pltpu.make_async_copy(w_hid_hbm, w_hid, load_sem.at[1])
    load_in.start()
    load_hid.start()

    barrier = pltpu.get_barrier_semaphore()
    for step in shard_bits + grp_bits:
        pl.semaphore_signal(barrier, inc=1, device_id=partner(step), device_id_type=MESH)
    for h in range(HALVES):
        gathered[h, 0] = table_ref[h * half : (h + 1) * half, :].astype(jnp.bfloat16)
    pl.semaphore_wait(barrier, len(shard_bits + grp_bits))

    started = []

    def send(source, target, send_sem, recv_sem, step):
        copy = pltpu.make_async_remote_copy(
            src_ref=source,
            dst_ref=target,
            send_sem=send_sem,
            recv_sem=recv_sem,
            device_id=partner(step),
            device_id_type=MESH,
        )
        copy.start()
        started.append(copy)
        return copy

    def gather_step(i):
        return [
            send(
                gathered.at[h, pl.ds(0, 1 << i)],
                gathered.at[h, pl.ds(1 << i, 1 << i)],
                gather_send.at[h, i],
                gather_recv.at[h, i],
                gather_order[h][i],
            )
            for h in range(HALVES)
        ]

    in_flight = gather_step(0)

    ids = owner_ref[...] * rows + row_ref[...]
    for j in range(SLOTS * HOT):
        keys[j] = jnp.broadcast_to(ids[:, j : j + 1], (samples, 128))

    lane = lax.broadcasted_iota(jnp.int32, (32, 128), 1)

    def build(h, place):
        relative = low_first(gather_order[h], place)["shard"]
        first = flip(me["shard"], relative) * rows + h * half
        block = counts.at[h * n_shard + place if keep else 0]

        def tile(t, _):
            at = pl.ds(pl.multiple_of(t * 32, 32), 32)
            for s in range(SLOTS):
                named = [keys[s * HOT + j, at, :] - first for j in range(HOT)]
                for c in range(half // 128):
                    hits = [jnp.where(k == lane + c * 128, 1.0, 0.0) for k in named]
                    total = (hits[0] + hits[1]) + (hits[2] + hits[3])
                    block[s, at, c * 128 : (c + 1) * 128] = total.astype(jnp.bfloat16)
            return 0

        lax.fori_loop(0, samples // 32, tile, 0)
        return block

    lookups[...] = jnp.zeros_like(lookups)

    def look_up(h, place, block):
        for s in range(SLOTS):
            lookups[s] += jnp.dot(
                block[s], gathered[h, place], preferred_element_type=jnp.float32
            )

    places = [(h, p) for p in range(n_shard) for h in range(HALVES)]
    steps = len(shard_bits)
    if keep:
        share = len(places) // steps
        for i in range(steps):
            end = len(places) if i == steps - 1 else (i + 1) * share
            for h, p in places[i * share : end]:
                build(h, p)
            for copy in in_flight:
                copy.wait_recv()
            if i < steps - 1:
                in_flight = gather_step(i + 1)
        for h, p in places:
            look_up(h, p, counts.at[h * n_shard + p])
    else:
        for i in range(steps):
            for copy in in_flight:
                copy.wait_recv()
            if i < steps - 1:
                in_flight = gather_step(i + 1)
        for h, p in places:
            look_up(h, p, build(h, p))

    for s in range(SLOTS):
        pooled[:, s * width : (s + 1) * width] = lookups[s].astype(jnp.bfloat16)
    columns = [slice(c, c + TILE) for c in range(0, hidden, TILE)]
    load_in.wait()
    for c in columns:
        value = jnp.dot(pooled[...], w_in[:, c], preferred_element_type=jnp.float32)
        pre_one[:, c] = value
        act_one[:, c] = jnp.maximum(value, 0.0).astype(jnp.bfloat16)
    load_hid.wait()
    out_row = w_out_ref[...].astype(jnp.float32)
    terms = jnp.zeros((samples, TILE), jnp.float32)
    for c in columns:
        value = jnp.dot(act_one[...], w_hid[:, c], preferred_element_type=jnp.float32)
        pre_two[:, c] = value
        acted = jnp.maximum(value, 0.0).astype(jnp.bfloat16).astype(jnp.float32)
        terms = terms + acted * out_row[:, c]
    logits = jnp.broadcast_to(jnp.sum(terms, axis=1, keepdims=True), (samples, 128))
    label = label_ref[...].astype(jnp.float32)
    batches, per_batch = label.shape
    label_columns = []
    for b in range(batches):
        at = slice(b * per_batch, (b + 1) * per_batch)
        logit_ref[b : b + 1, :] = jnp.transpose(logits[at, :])[0:1, :]
        label_columns.append(
            jnp.transpose(jnp.broadcast_to(label[b : b + 1, :], (128, per_batch)))
        )
    slope = (jax.nn.sigmoid(logits) - jnp.concatenate(label_columns, axis=0))[:, 0:1]
    for c in columns:
        back_two[:, c] = jnp.where(pre_two[:, c] > 0, slope * out_row[:, c], 0.0).astype(
            jnp.bfloat16
        )
    across = (((1,), (1,)), ((), ()))
    for c in columns:
        value = lax.dot_general(
            back_two[...], w_hid[c, :], across, preferred_element_type=jnp.float32
        )
        back_one[:, c] = jnp.where(pre_one[:, c] > 0, value, 0.0).astype(jnp.bfloat16)

    turned = jnp.transpose(pooled[...].astype(jnp.float32)).astype(jnp.bfloat16)
    total_ref = weight_term if scatter else weight_ref
    for c in columns:
        total_ref[:, c] = jnp.dot(turned, back_one[:, c], preferred_element_type=jnp.float32)

    weight_steps = len(weight_order) if scatter else 0
    chunks = 1 << weight_steps

    def weight_step(i):
        count = chunks >> (i + 1)
        at = pl.ds(chunks - 2 * count, count)
        return send(
            weight_out.at[at],
            weight_in.at[at],
            weight_send.at[i],
            weight_recv.at[i],
            weight_order[i],
        )

    def weight_add(i, copy):
        copy.wait_recv()
        count = chunks >> (i + 1)
        base = chunks - 2 * count
        weight_sum[0:count] += weight_in[base : base + count].astype(jnp.float32)
        if i < weight_steps - 1:
            left = count // 2
            weight_out[chunks - count : chunks - left] = weight_sum[left:count].astype(
                jnp.bfloat16
            )
            return weight_step(i + 1)
        return None

    weight_copy = None
    if scatter:
        depth = weight_sum.shape[1]

        def chunk_of(place):
            relative = high_first(weight_order, place)
            index = flip(me["grp"], relative["grp"]) * n_shard + flip(
                me["shard"], relative["shard"]
            )
            return weight_term[pl.ds(pl.multiple_of(index * depth, depth), depth), :]

        kept = chunks // 2
        for p in range(kept):
            weight_out[p] = chunk_of(kept + p).astype(jnp.bfloat16)
        weight_copy = weight_step(0)
        for p in range(kept):
            weight_sum[p] = chunk_of(p)

    back_in = [
        lax.dot_general(
            back_one[...],
            w_in[s * width : (s + 1) * width, :],
            across,
            preferred_element_type=jnp.float32,
        )
        .astype(jnp.bfloat16)
        .astype(jnp.float32)
        for s in range(SLOTS)
    ]
    back_turned = jnp.transpose(jnp.concatenate(back_in, axis=0)).astype(jnp.bfloat16)

    where_in = [
        {low_first(gather_order[h], p)["shard"]: p for p in range(n_shard)}
        for h in range(HALVES)
    ]

    def row_term(place, h):
        p = where_in[h][high_first(row_order, place)["shard"]]
        block = counts.at[h * n_shard + p] if keep else build(h, p)
        return jnp.dot(
            back_turned,
            block[...].reshape(SLOTS * samples, half),
            preferred_element_type=jnp.float32,
        )

    def row_step(i):
        count = n_shard >> (i + 1)
        at = pl.ds(n_shard - 2 * count, count)
        return send(row_out.at[at], row_in.at[at], row_send.at[i], row_recv.at[i], row_order[i])

    def row_add(i, copy):
        copy.wait_recv()
        count = n_shard >> (i + 1)
        base = n_shard - 2 * count
        row_sum[0:count] += row_in[base : base + count].astype(jnp.float32)
        left = count // 2
        if i < len(row_order) - 1:
            row_out[n_shard - count : n_shard - left] = row_sum[left:count].astype(jnp.bfloat16)
            return row_step(i + 1)
        return group_step(0)

    def group_step(i):
        place = n_shard - 1 + i
        row_out[place] = row_sum[0].astype(jnp.bfloat16)
        at = pl.ds(place, 1)
        k = len(row_order) + i
        return send(row_out.at[at], row_in.at[at], row_send.at[k], row_recv.at[k], grp_bits[i])

    def group_add(i, copy):
        copy.wait_recv()
        place = n_shard - 1 + i
        row_sum[0] = row_out[place].astype(jnp.float32) + row_in[place].astype(jnp.float32)
        return group_step(i + 1) if i < len(grp_bits) - 1 else None

    kept = n_shard // 2
    for p in range(kept):
        for h in range(HALVES):
            row_out[p, :, h * half : (h + 1) * half] = row_term(kept + p, h).astype(jnp.bfloat16)
    row_copy = row_step(0)
    for p in range(kept):
        for h in range(HALVES):
            row_sum[p, :, h * half : (h + 1) * half] = row_term(p, h)

    adds = [functools.partial(row_add, i) for i in range(len(row_order))]
    adds += [functools.partial(group_add, i) for i in range(len(grp_bits))]
    for i in range(max(len(adds), weight_steps)):
        if i < weight_steps:
            weight_copy = weight_add(i, weight_copy)
        if i < len(adds):
            row_copy = adds[i](row_copy)

    if scatter:
        lines = hidden // 128
        for j in range(lines):
            weight_ref[pl.ds(j, depth, stride=lines), :] = weight_sum[
                0, :, j * 128 : (j + 1) * 128
            ]
    grad = jnp.transpose(row_sum[0])
    new_sums = sums_ref[...] + grad * grad
    new_ref[...] = table_ref[...] - learn_rate * grad / jnp.sqrt(new_sums)
    for copy in started:
        copy.wait_send()


def local(
    n_shard,
    n_grp,
    owner_shard,
    local_row,
    click_label,
    row_table,
    squared_sums,
    w_input,
    w_hidden,
    w_output,
):
    rows, width = row_table.shape
    batches, per_batch, looks = local_row.shape
    samples = batches * per_batch
    wide, hidden = w_input.shape
    depth = wide // (n_shard * n_grp)
    scatter = depth > 0 and depth % 16 == 0
    keep = n_shard <= 8
    half = rows // HALVES
    chunks = n_shard * n_grp if scatter else 1
    depth = depth if scatter else 16
    shard_steps = n_shard.bit_length() - 1
    grp_steps = n_grp.bit_length() - 1
    row_slots = n_shard - 1 + grp_steps
    vmem = pl.BlockSpec(memory_space=pltpu.VMEM)
    hbm = pl.BlockSpec(memory_space=pl.ANY)
    low = jnp.bfloat16
    full = jnp.float32
    weight_shape = (depth * hidden // 128, 128) if scatter else (wide, hidden)
    new_table, logits, weight = pl.pallas_call(
        functools.partial(kernel, n_shard, n_grp, keep, scatter),
        out_shape=(
            jax.ShapeDtypeStruct((rows, width), full),
            jax.ShapeDtypeStruct((batches, per_batch), full),
            jax.ShapeDtypeStruct(weight_shape, full),
        ),
        in_specs=[vmem, vmem, vmem, vmem, vmem, hbm, hbm, vmem],
        out_specs=(vmem, vmem, vmem),
        scratch_shapes=[
            pltpu.VMEM((wide, hidden), low),
            pltpu.VMEM((hidden, hidden), low),
            pltpu.VMEM((HALVES, n_shard, half, width), low),
            pltpu.VMEM((looks, samples, 128), jnp.int32),
            pltpu.VMEM((HALVES * n_shard if keep else 1, SLOTS, samples, half), low),
            pltpu.VMEM((SLOTS, samples, width), full),
            pltpu.VMEM((samples, wide), low),
            pltpu.VMEM((samples, hidden), full),
            pltpu.VMEM((samples, hidden), low),
            pltpu.VMEM((samples, hidden), full),
            pltpu.VMEM((16, 128), low),
            pltpu.VMEM((samples, hidden), low),
            pltpu.VMEM((samples, hidden), low),
            pltpu.VMEM((n_shard // 2, width, rows), full),
            pltpu.VMEM((row_slots, width, rows), low),
            pltpu.VMEM((row_slots, width, rows), low),
            pltpu.VMEM((wide, hidden) if scatter else (8, 128), full),
            pltpu.VMEM((max(1, chunks // 2), depth, hidden), full),
            pltpu.VMEM((max(1, chunks - 1), depth, hidden), low),
            pltpu.VMEM((max(1, chunks - 1), depth, hidden), low),
            pltpu.SemaphoreType.DMA((2,)),
            pltpu.SemaphoreType.DMA((HALVES, shard_steps)),
            pltpu.SemaphoreType.DMA((HALVES, shard_steps)),
            pltpu.SemaphoreType.DMA((shard_steps + grp_steps,)),
            pltpu.SemaphoreType.DMA((shard_steps + grp_steps,)),
            pltpu.SemaphoreType.DMA((shard_steps + grp_steps,)),
            pltpu.SemaphoreType.DMA((shard_steps + grp_steps,)),
        ],
        compiler_params=pltpu.CompilerParams(
            collective_id=0, has_side_effects=True, vmem_limit_bytes=56 * 1024 * 1024
        ),
    )(
        owner_shard.reshape(samples, looks),
        local_row.reshape(samples, looks),
        click_label,
        row_table,
        squared_sums,
        w_input,
        w_hidden,
        w_output.reshape(1, hidden),
    )
    weight = weight.reshape(-1)
    if not scatter:
        weight = lax.psum_scatter(weight, ("grp", "shard"), scatter_dimension=0, tiled=True)
    return (new_table, logits, weight)


def solution(mesh):
    in_specs = (
        P(None, ("grp", "shard"), None, None),
        P(None, ("grp", "shard"), None),
        P(None, ("grp", "shard")),
        P("shard", None),
        P("shard", None),
        P(),
        P(),
        P(),
    )
    out_specs = (P("shard", None), P(None, ("grp", "shard")), P(("grp", "shard")))
    part = functools.partial(local, mesh.shape["shard"], mesh.shape["grp"])
    return jax.shard_map(part, mesh=mesh, in_specs=in_specs, out_specs=out_specs, check_vma=False)
```

time: 283 us -> 59.2 us (0.21)
  waiting for transfers between devices: 219 us -> 0 us
  Pallas kernels: 0 us -> 49.6 us
  other arithmetic: 23.7 us -> 0 us
  matrix products: 17.6 us -> 0 us
  between operations: 13.9 us -> 0.64 us
    unnamed x5 -> x0, waiting for transfers between devices: 138 us -> none
    pallas_call x0 -> x1, Pallas kernels: none -> 49.6 us  [local(): pl.pallas_call(functools.partial(kernel, n_shard, n_grp, keep, scatter),...]
    reduce_scatter x1 -> x0, waiting for transfers between devices: 38.1 us -> none  [local(): lax.psum_scatter(row_part, 'shard', scatter_dimension=0, tiled=True)]
    psum x1 -> x0, waiting for transfers between devices: 34.7 us -> none  [local(): total = lax.psum(row_grad.astype(jnp.bfloat16), 'grp').astype(jnp.float32)]
    dot_general x8 -> x0, matrix products: 17.6 us -> none  [the longest x1 7.13 us: local(): lax.dot_general(counts, back_in.reshape(-1, width), (((0,), (0,)), ((), (...]
    reduce_sum x1 -> x0, other arithmetic: 17.2 us -> none  [local(): jnp.sum((ids[:, :, None] == rows[None, None, :]).astype(jnp.float32), axi...]
    all_gather x1 -> x0, waiting for transfers between devices: 7.89 us -> none  [local(): lax.all_gather(row_table.astype(jnp.bfloat16), 'shard', axis=0, tiled=True)]
    convert_element_type x3 -> x0, other arithmetic: 4.06 us -> none  [the longest x1 1.76 us: local(): row_table.astype(jnp.bfloat16)]
  transfers between devices with their start and end apart: 4 -> 0, of which waited for: 4 -> 0; matrix products, arithmetic and copies ran while one was open for 9% -> 0% of each run, Pallas kernels for 0% -> 0%
where the time goes in v2:
time: 59.2 us; the launch traced here: 58.8 us
  Pallas kernels  49.6 us (84%)
  local copies, waits for them, and re-layouts  8.61 us (15%)
  between operations  0.64 us (1%)
    pallas_call x1, Pallas kernels, local(): pl.pallas_call(functools.partial(kernel, n_shard, n_grp, keep, scatter),...  49.6 us
    unnamed x5, local copies, waits for them, and re-layouts  7.33 us
    reshape x1, local copies, waits for them, and re-layouts, local(): w_output.reshape(1, hidden)  1.28 us

profile of v2, /device:TPU:0, one launch (start us, length us, event | category | flops | bytes accessed | tf_op | source)
XLA Modules:
  0.0 58.8 jit_solution(7217934183037333771)
XLA Ops:
  0.6 1.3 %reshape.20.w_out_ref = bf16[1,1024]{1,0:T(2,128)(2,1)} reshape(bf16[1024]{0:T(1024)(128)(2,1)} %param.15) | data formatting | bytes 4096 | tf_op jit(solution)/shard_map/reshape | solution.py:453
  1.9 1.5 %copy.11 = s32[2,128,16,1]{2,1,0,3:T(8,128)} copy(s32[2,128,16,1]{1,3,2,0:T(1,128)} %param.8) | data formatting | bytes 32768 | tf_op args[0]
  3.4 1.5 %copy.12 = s32[2,128,16]{2,1,0:T(8,128)} copy(s32[2,128,16]{1,2,0:T(8,128)} %param.9) | data formatting | bytes 32768 | tf_op args[1]
  4.9 49.6 %shard_map.103 = (f32[512,128]{1,0:T(8,128)}, f32[2,128]{1,0:T(2,128)}, f32[128,128]{1,0:T(8,128)}) custom-call(s32[256,16]{1,0:T(8,128)} %bitcast.3, s32[256,16]{1,0:T(8,128)} %bitcast.4, s32[2,128]{1,0:T(2,128)} %label_ref.1, f32[512,128]{1,0:T(8,128)} %table_ref.1, f32[512,128]{1,0:T(8,128)} %sums_ref.1, bf16[512,1024]{1,0:T(8,128)(2,1)} %w_in_hbm.1, ...), custom_call_target="tpu_custom_call" | custom-call | tf_op jit(solution)/shard_map/pallas_call | solution.py:404
  54.4 1.7 %copy.16 = f32[512,128]{1,0:T(8,128)} copy(f32[512,128]{1,0:T(8,128)} %get-tuple-element.12) | data formatting | bytes 524288
  56.1 1.2 %copy.17 = f32[2,128]{1,0:T(2,128)} copy(f32[2,128]{1,0:T(2,128)} %get-tuple-element.13) | data formatting | bytes 2048
  57.4 1.5 %copy.18 = f32[16384]{0:T(1024)} copy(f32[16384]{0:T(1024)} %bitcast.5) | data formatting | bytes 131072

commit v3 on v2

--- a/solution.py
+++ b/solution.py
@@ -67,12 +67,15 @@
     pre_one,
     act_one,
     pre_two,
-    act_two,
     back_two,
     back_one,
     row_sum,
     row_out,
     row_in,
+    grad,
+    part_out,
+    part_in,
+    part_all,
     weight_term,
     weight_sum,
     weight_out,
@@ -82,10 +85,14 @@
     gather_recv,
     row_send,
     row_recv,
+    part_send,
+    part_recv,
     weight_send,
     weight_recv,
 ):
-    samples = owner_ref.shape[0]
+    looks = SLOTS * HOT
+    batches, per_batch = label_ref.shape
+    samples = batches * per_batch
     rows, width = table_ref.shape
     hidden = w_hid.shape[0]
     half = rows // HALVES
@@ -95,7 +102,7 @@
     near, far = shard_bits[:1], shard_bits[1:]
     gather_order = [far[::-1] + near, far + near]
     row_order = near + far
-    weight_order = near + far[::-1] + grp_bits[::-1]
+    weight_order = near + far[::-1] + grp_bits
 
     def partner(step):
         axis, bit = step
@@ -107,11 +114,12 @@
     load_hid.start()
 
     barrier = pltpu.get_barrier_semaphore()
-    for step in shard_bits + grp_bits:
+    peers = [("grp", relative) for relative in range(1, n_grp)]
+    for step in shard_bits + peers:
         pl.semaphore_signal(barrier, inc=1, device_id=partner(step), device_id_type=MESH)
     for h in range(HALVES):
         gathered[h, 0] = table_ref[h * half : (h + 1) * half, :].astype(jnp.bfloat16)
-    pl.semaphore_wait(barrier, len(shard_bits + grp_bits))
+    pl.semaphore_wait(barrier, len(shard_bits + peers))
 
     started = []
 
@@ -143,24 +151,31 @@
     in_flight = gather_step(0)
 
     ids = owner_ref[...] * rows + row_ref[...]
-    for j in range(SLOTS * HOT):
-        keys[j] = jnp.broadcast_to(ids[:, j : j + 1], (samples, 128))
+    for b in range(batches):
+        turned_ids = jnp.transpose(ids[b * looks : (b + 1) * looks, :])
+        for j in range(looks):
+            keys[j, b * per_batch : (b + 1) * per_batch, :] = jnp.broadcast_to(
+                turned_ids[:, j : j + 1], (per_batch, 128)
+            ).astype(jnp.int16)
 
     lane = lax.broadcasted_iota(jnp.int32, (32, 128), 1)
+    one = jnp.ones((32, 128), jnp.bfloat16)
+    none = jnp.zeros((32, 128), jnp.bfloat16)
 
     def build(h, place):
         relative = low_first(gather_order[h], place)["shard"]
         first = flip(me["shard"], relative) * rows + h * half
         block = counts.at[h * n_shard + place if keep else 0]
+        lanes = [(lane + (first + c * 128)).astype(jnp.int16) for c in range(half // 128)]
 
         def tile(t, _):
             at = pl.ds(pl.multiple_of(t * 32, 32), 32)
             for s in range(SLOTS):
-                named = [keys[s * HOT + j, at, :] - first for j in range(HOT)]
+                named = [keys[s * HOT + j, at, :] for j in range(HOT)]
                 for c in range(half // 128):
-                    hits = [jnp.where(k == lane + c * 128, 1.0, 0.0) for k in named]
+                    hits = [jnp.where(k == lanes[c], one, none) for k in named]
                     total = (hits[0] + hits[1]) + (hits[2] + hits[3])
-                    block[s, at, c * 128 : (c + 1) * 128] = total.astype(jnp.bfloat16)
+                    block[s, at, c * 128 : (c + 1) * 128] = total
             return 0
 
         lax.fori_loop(0, samples // 32, tile, 0)
@@ -206,7 +221,8 @@
         pre_one[:, c] = value
         act_one[:, c] = jnp.maximum(value, 0.0).astype(jnp.bfloat16)
     load_hid.wait()
-    out_row = w_out_ref[...].astype(jnp.float32)
+    out_lines = w_out_ref[...].astype(jnp.float32)
+    out_row = jnp.concatenate([out_lines[i : i + 1, :] for i in range(hidden // 128)], axis=1)
     terms = jnp.zeros((samples, TILE), jnp.float32)
     for c in columns:
         value = jnp.dot(act_one[...], w_hid[:, c], preferred_element_type=jnp.float32)
@@ -215,7 +231,6 @@
         terms = terms + acted * out_row[:, c]
     logits = jnp.broadcast_to(jnp.sum(terms, axis=1, keepdims=True), (samples, 128))
     label = label_ref[...].astype(jnp.float32)
-    batches, per_batch = label.shape
     label_columns = []
     for b in range(batches):
         at = slice(b * per_batch, (b + 1) * per_batch)
@@ -326,20 +341,46 @@
         if i < len(row_order) - 1:
             row_out[n_shard - count : n_shard - left] = row_sum[left:count].astype(jnp.bfloat16)
             return row_step(i + 1)
-        return group_step(0)
-
-    def group_step(i):
-        place = n_shard - 1 + i
-        row_out[place] = row_sum[0].astype(jnp.bfloat16)
-        at = pl.ds(place, 1)
-        k = len(row_order) + i
-        return send(row_out.at[at], row_in.at[at], row_send.at[k], row_recv.at[k], grp_bits[i])
-
-    def group_add(i, copy):
-        copy.wait_recv()
-        place = n_shard - 1 + i
-        row_sum[0] = row_out[place].astype(jnp.float32) + row_in[place].astype(jnp.float32)
-        return group_step(i + 1) if i < len(grp_bits) - 1 else None
+        return group_send()
+
+    part = rows // n_grp
+
+    def rows_of(relative):
+        at = flip(me["grp"], relative) * part
+        return pl.ds(pl.multiple_of(at, part), part)
+
+    def group_send():
+        grad[...] = jnp.transpose(row_sum[0])
+        copies = []
+        for i, step in enumerate(peers):
+            part_out[i] = grad[rows_of(step[1]), :].astype(jnp.bfloat16)
+            copies.append(
+                send(
+                    part_out.at[i],
+                    part_in.at[i],
+                    part_send.at[0, i],
+                    part_recv.at[0, i],
+                    step,
+                )
+            )
+        return copies
+
+    def group_sum(copies):
+        total = grad[rows_of(0), :]
+        for i, copy in enumerate(copies):
+            copy.wait_recv()
+            total = total + part_in[i].astype(jnp.float32)
+        part_all[0] = total.astype(jnp.bfloat16)
+        return [
+            send(
+                part_all.at[0],
+                part_all.at[step[1]],
+                part_send.at[1, i],
+                part_recv.at[1, i],
+                step,
+            )
+            for i, step in enumerate(peers)
+        ]
 
     kept = n_shard // 2
     for p in range(kept):
@@ -350,13 +391,16 @@
         for h in range(HALVES):
             row_sum[p, :, h * half : (h + 1) * half] = row_term(p, h)
 
-    adds = [functools.partial(row_add, i) for i in range(len(row_order))]
-    adds += [functools.partial(group_add, i) for i in range(len(grp_bits))]
-    for i in range(max(len(adds), weight_steps)):
-        if i < weight_steps:
+    for i in range(len(row_order)):
+        if scatter:
             weight_copy = weight_add(i, weight_copy)
-        if i < len(adds):
-            row_copy = adds[i](row_copy)
+        row_copy = row_add(i, row_copy)
+    weight_left = list(range(len(row_order), weight_steps))
+    for i in weight_left[:1]:
+        weight_copy = weight_add(i, weight_copy)
+    row_copy = group_sum(row_copy)
+    for i in weight_left[1:]:
+        weight_copy = weight_add(i, weight_copy)
 
     if scatter:
         lines = hidden // 128
@@ -364,9 +408,13 @@
             weight_ref[pl.ds(j, depth, stride=lines), :] = weight_sum[
                 0, :, j * 128 : (j + 1) * 128
             ]
-    grad = jnp.transpose(row_sum[0])
-    new_sums = sums_ref[...] + grad * grad
-    new_ref[...] = table_ref[...] - learn_rate * grad / jnp.sqrt(new_sums)
+    for i in range(n_grp):
+        if i > 0:
+            row_copy[i - 1].wait_recv()
+        at = rows_of(i)
+        term = part_all[i].astype(jnp.float32)
+        new_sums = sums_ref[at, :] + term * term
+        new_ref[at, :] = table_ref[at, :] - learn_rate * term / jnp.sqrt(new_sums)
     for copy in started:
         copy.wait_send()
 
@@ -395,7 +443,7 @@
     depth = depth if scatter else 16
     shard_steps = n_shard.bit_length() - 1
     grp_steps = n_grp.bit_length() - 1
-    row_slots = n_shard - 1 + grp_steps
+    part = rows // n_grp
     vmem = pl.BlockSpec(memory_space=pltpu.VMEM)
     hbm = pl.BlockSpec(memory_space=pl.ANY)
     low = jnp.bfloat16
@@ -414,19 +462,22 @@
             pltpu.VMEM((wide, hidden), low),
             pltpu.VMEM((hidden, hidden), low),
             pltpu.VMEM((HALVES, n_shard, half, width), low),
-            pltpu.VMEM((looks, samples, 128), jnp.int32),
+            pltpu.VMEM((looks, samples, 128), jnp.int16),
             pltpu.VMEM((HALVES * n_shard if keep else 1, SLOTS, samples, half), low),
             pltpu.VMEM((SLOTS, samples, width), full),
             pltpu.VMEM((samples, wide), low),
             pltpu.VMEM((samples, hidden), full),
             pltpu.VMEM((samples, hidden), low),
             pltpu.VMEM((samples, hidden), full),
-            pltpu.VMEM((16, 128), low),
             pltpu.VMEM((samples, hidden), low),
             pltpu.VMEM((samples, hidden), low),
             pltpu.VMEM((n_shard // 2, width, rows), full),
-            pltpu.VMEM((row_slots, width, rows), low),
-            pltpu.VMEM((row_slots, width, rows), low),
+            pltpu.VMEM((n_shard - 1, width, rows), low),
+            pltpu.VMEM((n_shard - 1, width, rows), low),
+            pltpu.VMEM((rows, width), full),
+            pltpu.VMEM((n_grp - 1, part, width), low),
+            pltpu.VMEM((n_grp - 1, part, width), low),
+            pltpu.VMEM((n_grp, part, width), low),
             pltpu.VMEM((wide, hidden) if scatter else (8, 128), full),
             pltpu.VMEM((max(1, chunks // 2), depth, hidden), full),
             pltpu.VMEM((max(1, chunks - 1), depth, hidden), low),
@@ -434,8 +485,10 @@
             pltpu.SemaphoreType.DMA((2,)),
             pltpu.SemaphoreType.DMA((HALVES, shard_steps)),
             pltpu.SemaphoreType.DMA((HALVES, shard_steps)),
-            pltpu.SemaphoreType.DMA((shard_steps + grp_steps,)),
-            pltpu.SemaphoreType.DMA((shard_steps + grp_steps,)),
+            pltpu.SemaphoreType.DMA((shard_steps,)),
+            pltpu.SemaphoreType.DMA((shard_steps,)),
+            pltpu.SemaphoreType.DMA((2, n_grp - 1)),
+            pltpu.SemaphoreType.DMA((2, n_grp - 1)),
             pltpu.SemaphoreType.DMA((shard_steps + grp_steps,)),
             pltpu.SemaphoreType.DMA((shard_steps + grp_steps,)),
         ],
@@ -443,14 +496,14 @@
             collective_id=0, has_side_effects=True, vmem_limit_bytes=56 * 1024 * 1024
         ),
     )(
-        owner_shard.reshape(samples, looks),
-        local_row.reshape(samples, looks),
+        jnp.transpose(owner_shard, (0, 2, 3, 1)).reshape(batches * looks, per_batch),
+        jnp.transpose(local_row, (0, 2, 1)).reshape(batches * looks, per_batch),
         click_label,
         row_table,
         squared_sums,
         w_input,
         w_hidden,
-        w_output.reshape(1, hidden),
+        w_output.reshape(hidden // 128, 128),
     )
     weight = weight.reshape(-1)
     if not scatter:

time: 59.2 us -> 52.6 us (0.89)
  local copies, waits for them, and re-layouts: 8.61 us -> 4.38 us
  Pallas kernels: 49.6 us -> 47.4 us
    unnamed x5 -> x3, local copies, waits for them, and re-layouts: 7.33 us -> 4.38 us
    pallas_call x1, Pallas kernels: 49.6 us -> 47.4 us  [local(): pl.pallas_call(functools.partial(kernel, n_shard, n_grp, keep, scatter),...]
    reshape x1 -> x0, local copies, waits for them, and re-layouts: 1.28 us -> none  [local(): w_output.reshape(1, hidden)]
where the time goes in v3:
time: 52.6 us; the launch traced here: 52.4 us
  Pallas kernels  47.4 us (90%)
  local copies, waits for them, and re-layouts  4.38 us (8%)
  between operations  0.64 us (1%)
    pallas_call x1, Pallas kernels, local(): pl.pallas_call(functools.partial(kernel, n_shard, n_grp, keep, scatter),...  47.4 us
    unnamed x3, local copies, waits for them, and re-layouts  4.38 us

profile of v3, /device:TPU:0, one launch (start us, length us, event | category | flops | bytes accessed | tf_op | source)
XLA Modules:
  0.0 52.4 jit_solution(8728378829588157191)
XLA Ops:
  0.6 47.4 %shard_map.103 = (f32[512,128]{1,0:T(8,128)}, f32[2,128]{1,0:T(2,128)}, f32[128,128]{1,0:T(8,128)}) custom-call(s32[32,128]{1,0:T(8,128)} %bitcast.9, s32[32,128]{1,0:T(8,128)} %bitcast.10, s32[2,128]{1,0:T(2,128)} %label_ref.1, f32[512,128]{1,0:T(8,128)} %table_ref.1, f32[512,128]{1,0:T(8,128)} %sums_ref.1, bf16[512,1024]{1,0:T(8,128)(2,1)} %w_in_hbm.1, ...), custom_call_target="tpu_custom_call" | custom-call | tf_op jit(solution)/shard_map/pallas_call | solution.py:452
  48.0 1.7 %copy.14 = f32[512,128]{1,0:T(8,128)} copy(f32[512,128]{1,0:T(8,128)} %get-tuple-element.12) | data formatting | bytes 524288
  49.7 1.2 %copy.15 = f32[2,128]{1,0:T(2,128)} copy(f32[2,128]{1,0:T(2,128)} %get-tuple-element.13) | data formatting | bytes 2048
  50.9 1.5 %copy.16 = f32[16384]{0:T(1024)} copy(f32[16384]{0:T(1024)} %bitcast.8) | data formatting | bytes 131072

commit v4 on v3

--- a/solution.py
+++ b/solution.py
@@ -62,7 +62,6 @@
     gathered,
     keys,
     counts,
-    lookups,
     pooled,
     pre_one,
     act_one,
@@ -165,29 +164,23 @@
     def build(h, place):
         relative = low_first(gather_order[h], place)["shard"]
         first = flip(me["shard"], relative) * rows + h * half
-        block = counts.at[h * n_shard + place if keep else 0]
+        left = (h * n_shard + place) * half if keep else 0
+        block = counts.at[:, left : left + half]
         lanes = [(lane + (first + c * 128)).astype(jnp.int16) for c in range(half // 128)]
 
         def tile(t, _):
             at = pl.ds(pl.multiple_of(t * 32, 32), 32)
             for s in range(SLOTS):
+                into = pl.ds(pl.multiple_of(s * samples + t * 32, 32), 32)
                 named = [keys[s * HOT + j, at, :] for j in range(HOT)]
                 for c in range(half // 128):
                     hits = [jnp.where(k == lanes[c], one, none) for k in named]
                     total = (hits[0] + hits[1]) + (hits[2] + hits[3])
-                    block[s, at, c * 128 : (c + 1) * 128] = total
+                    counts[into, left + c * 128 : left + (c + 1) * 128] = total
             return 0
 
         lax.fori_loop(0, samples // 32, tile, 0)
         return block
-
-    lookups[...] = jnp.zeros_like(lookups)
-
-    def look_up(h, place, block):
-        for s in range(SLOTS):
-            lookups[s] += jnp.dot(
-                block[s], gathered[h, place], preferred_element_type=jnp.float32
-            )
 
     places = [(h, p) for p in range(n_shard) for h in range(HALVES)]
     steps = len(shard_bits)
@@ -201,19 +194,27 @@
                 copy.wait_recv()
             if i < steps - 1:
                 in_flight = gather_step(i + 1)
-        for h, p in places:
-            look_up(h, p, counts.at[h * n_shard + p])
+        lookups = jnp.dot(
+            counts[...],
+            gathered[...].reshape(HALVES * n_shard * half, width),
+            preferred_element_type=jnp.float32,
+        )
     else:
         for i in range(steps):
             for copy in in_flight:
                 copy.wait_recv()
             if i < steps - 1:
                 in_flight = gather_step(i + 1)
+        lookups = jnp.zeros((SLOTS * samples, width), jnp.float32)
         for h, p in places:
-            look_up(h, p, build(h, p))
+            lookups += jnp.dot(
+                build(h, p)[...], gathered[h, p], preferred_element_type=jnp.float32
+            )
 
     for s in range(SLOTS):
-        pooled[:, s * width : (s + 1) * width] = lookups[s].astype(jnp.bfloat16)
+        pooled[:, s * width : (s + 1) * width] = lookups[
+            s * samples : (s + 1) * samples
+        ].astype(jnp.bfloat16)
     columns = [slice(c, c + TILE) for c in range(0, hidden, TILE)]
     load_in.wait()
     for c in columns:
@@ -320,10 +321,11 @@
 
     def row_term(place, h):
         p = where_in[h][high_first(row_order, place)["shard"]]
-        block = counts.at[h * n_shard + p] if keep else build(h, p)
+        left = (h * n_shard + p) * half
+        block = counts.at[:, left : left + half] if keep else build(h, p)
         return jnp.dot(
             back_turned,
-            block[...].reshape(SLOTS * samples, half),
+            block[...],
             preferred_element_type=jnp.float32,
         )
 
@@ -417,6 +419,18 @@
         new_ref[at, :] = table_ref[at, :] - learn_rate * term / jnp.sqrt(new_sums)
     for copy in started:
         copy.wait_send()
+
+
+def hand_over(*refs):
+    sources, targets, sems = refs[:3], refs[3:6], refs[6]
+    copies = [
+        pltpu.make_async_copy(source, target, sems.at[i])
+        for i, (source, target) in enumerate(zip(sources, targets))
+    ]
+    for copy in copies:
+        copy.start()
+    for copy in copies:
+        copy.wait()
 
 
 def local(
@@ -463,8 +477,7 @@
             pltpu.VMEM((hidden, hidden), low),
             pltpu.VMEM((HALVES, n_shard, half, width), low),
             pltpu.VMEM((looks, samples, 128), jnp.int16),
-            pltpu.VMEM((HALVES * n_shard if keep else 1, SLOTS, samples, half), low),
-            pltpu.VMEM((SLOTS, samples, width), full),
+            pltpu.VMEM((SLOTS * samples, HALVES * n_shard * half if keep else half), low),
             pltpu.VMEM((samples, wide), low),
             pltpu.VMEM((samples, hidden), full),
             pltpu.VMEM((samples, hidden), low),
@@ -505,6 +518,17 @@
         w_hidden,
         w_output.reshape(hidden // 128, 128),
     )
+    if scatter:
+        new_table, logits, weight = pl.pallas_call(
+            hand_over,
+            out_shape=tuple(
+                jax.ShapeDtypeStruct(a.shape, a.dtype) for a in (new_table, logits, weight)
+            ),
+            in_specs=[hbm, hbm, hbm],
+            out_specs=(hbm, hbm, hbm),
+            scratch_shapes=[pltpu.SemaphoreType.DMA((3,))],
+            compiler_params=pltpu.CompilerParams(vmem_limit_bytes=60 * 1024 * 1024),
+        )(new_table, logits, weight)
     weight = weight.reshape(-1)
     if not scatter:
         weight = lax.psum_scatter(weight, ("grp", "shard"), scatter_dimension=0, tiled=True)

time: 52.6 us -> 63.6 us (1.21)
  Pallas kernels: 47.4 us -> 62.8 us
  local copies, waits for them, and re-layouts: 4.38 us -> 0 us
    pallas_call x0 -> x1, Pallas kernels: none -> 11.1 us  [local(): pl.pallas_call(hand_over, out_shape=tuple((jax.ShapeDtypeStruct(a.shape,...]
    unnamed x3 -> x0, local copies, waits for them, and re-layouts: 4.38 us -> none
    pallas_call x1, Pallas kernels: 47.4 us -> 51.7 us  [local(): pl.pallas_call(functools.partial(kernel, n_shard, n_grp, keep, scatter),...]
where the time goes in v4:
time: 63.6 us; the launch traced here: 63.4 us
  Pallas kernels  62.8 us (99%)
  between operations  0.64 us (1%)
    pallas_call x1, Pallas kernels, local(): pl.pallas_call(functools.partial(kernel, n_shard, n_grp, keep, scatter),...  51.7 us
    pallas_call x1, Pallas kernels, local(): pl.pallas_call(hand_over, out_shape=tuple((jax.ShapeDtypeStruct(a.shape,...  11.1 us

profile of v4, /device:TPU:0, one launch (start us, length us, event | category | flops | bytes accessed | tf_op | source)
XLA Modules:
  0.0 63.4 jit_solution(14441319001299992586)
XLA Ops:
  0.6 51.7 %shard_map.103 = (f32[512,128]{1,0:T(8,128)}, f32[2,128]{1,0:T(2,128)}, f32[128,128]{1,0:T(8,128)}) custom-call(s32[32,128]{1,0:T(8,128)} %bitcast.8, s32[32,128]{1,0:T(8,128)} %bitcast.9, s32[2,128]{1,0:T(2,128)} %label_ref.1, f32[512,128]{1,0:T(8,128)} %table_ref.1, f32[512,128]{1,0:T(8,128)} %sums_ref.1, bf16[512,1024]{1,0:T(8,128)(2,1)} %w_in_hbm.1, ...), custom_call_target="tpu_custom_call" | custom-call | tf_op jit(solution)/shard_map/pallas_call | solution.py:466
  52.3 11.1 %shard_map.104 = (f32[512,128]{1,0:T(8,128)}, f32[2,128]{1,0:T(2,128)}, f32[128,128]{1,0:T(8,128)}) custom-call(f32[512,128]{1,0:T(8,128)} %get-tuple-element.9.refs_0_, f32[2,128]{1,0:T(2,128)} %get-tuple-element.10.refs_1_, f32[128,128]{1,0:T(8,128)} %get-tuple-element.11.refs_2_), custom_call_target="tpu_custom_call" | custom-call | tf_op jit(solution)/shard_map/pallas_call | solution.py:522
